TPU v7x, 128 devices: a whole 4x4x4 slice. The times are simulated.
128 devices in a mesh: space: 32 (over z, y, core), orb: 4 (over x).
Axes of the slice: x: 4, y: 4, z: 4, core: 2. Of those that a mesh axis runs over, the one named last changes fastest.
Arguments:
- orbitals: float32 [8, 32768, 256], P('orb', 'space'), may hold values from -6 to 6
- near_source: int32 [32768, 27], P('space'), may hold values from 0 to 32767, as said below
- far_leaf: int32 [32768, 108], P('space'), may hold values from 0 to 32767, as said below
- far_mid: int32 [4096, 108], P('space'), may hold values from 0 to 4095, as said below
- far_top: int32 [512, 108], P('space'), may hold values from 0 to 511, as said below
- leaf_basis: bfloat16 [64, 256], replicated, may hold values from -0.375 to 0.375
- near_table: bfloat16 [27, 256, 256], replicated, may hold values from -0.078125 to 0.078125
- transfer: bfloat16 [8, 64, 64], replicated, may hold values from -0.75 to 0.75
- coupling: bfloat16 [108, 64, 64], replicated, may hold values from -0.078125 to 0.078125
- pair_transfer: bfloat16 [2, 64, 64], replicated, may hold values from -0.75 to 0.75
- coarse_coupling: bfloat16 [4, 64, 64], replicated, may hold values from -0.4375 to 0.4375
Outputs:
- relaxed: float32 [8, 32768, 256], P('orb', 'space')
Inputs may be any that keep to these rules, and one draw needn't show every extreme that they name: `near_source`: with layer(t) = t // 64: every entry of leaf t lies in a layer at most 1 from layer(t); entry 13 is t itself; entry 0 is the leaf at t's transverse position one layer away. `far_leaf`: with layer(t) = t // 64: every entry of box t lies in a layer 2 or 3 away from layer(t); entry 0 is exactly 3 layers away. `far_mid`: with layer(t) = t // 16: every entry of box t lies in a layer 2 or 3 away from layer(t); entry 0 is exactly 3 layers away. `far_top`: with layer(t) = t // 4: every entry of box t lies in a layer 2 or 3 away from layer(t); entry 0 is exactly 3 layers away.
All inputs are finite; a program needn't handle non-finite values.
Results may differ from a plain program's by a relative error of at most 0.012.
Values may be sent and summed in bfloat16 or wider, within the bound.
A program may use at most 192 MiB of HBM per device.

v0:
```python
import jax
import jax.numpy as jnp
from jax import lax
from jax.sharding import PartitionSpec as P

SIDE = 8
relax_step = 0.1


def padded(cells, sides, width):
    for axis, dim in sides:
        count = lax.axis_size(axis)
        ends = count - 1
        head = lax.slice_in_dim(cells, 0, width, axis=dim)
        tail = lax.slice_in_dim(cells, cells.shape[dim] - width, cells.shape[dim], axis=dim)
        cells = jnp.concatenate(
            [
                lax.ppermute(tail, axis, [(i, (i + 1) % count) for i in range(ends)]),
                cells,
                lax.ppermute(head, axis, [((i + 1) % count, i) for i in range(ends)]),
            ],
            axis=dim,
        )
    return cells


def leaf_project(density, leaf_basis):
    return jnp.einsum(
        "olp,rp->lor", density, leaf_basis, preferred_element_type=jnp.float32
    ).astype(jnp.bfloat16)


def octant_up(moments, side_boxes, transfer):
    node_count, orbits, rank_width = moments.shape
    layers = node_count // (side_boxes * side_boxes)
    half_side = side_boxes // 2
    shaped = moments.reshape(layers // 2, 2, half_side, 2, half_side, 2, orbits, rank_width)
    octant_grid = transfer.reshape(2, 2, 2, rank_width, rank_width)
    parents = jnp.einsum(
        "apbqcuos,pqusr->abcor", shaped, octant_grid, preferred_element_type=jnp.float32
    )
    return parents.reshape(-1, orbits, rank_width).astype(jnp.bfloat16)


def octant_down(coeffs, side_boxes, transfer):
    node_count, orbits, rank_width = coeffs.shape
    layers = node_count // (side_boxes * side_boxes)
    shaped = coeffs.reshape(layers, side_boxes, side_boxes, orbits, rank_width)
    octant_grid = transfer.reshape(2, 2, 2, rank_width, rank_width)
    children = jnp.einsum(
        "abcor,pqusr->apbqcuos", shaped, octant_grid, preferred_element_type=jnp.float32
    )
    return children.reshape(-1, orbits, rank_width)


def couple_rows(moments, sources, coupling, scale):
    node_count, orbits, rank_width = moments.shape
    flattened = moments.reshape(node_count, orbits * rank_width)
    identity = jnp.eye(orbits, dtype=coupling.dtype)
    running = None
    for column_start in range(0, sources.shape[1], 27):
        block_coupling = coupling[column_start : column_start + 27]
        widened = jnp.einsum("ab,krs->kasbr", identity, block_coupling).reshape(
            block_coupling.shape[0], orbits * rank_width, orbits * rank_width
        )
        picked = jnp.take(flattened, sources[:, column_start : column_start + 27], axis=0)
        piece_sum = jnp.einsum("lkx,kxy->ly", picked, widened, preferred_element_type=jnp.float32)
        running = piece_sum if running is None else running + piece_sum
    return scale * running.reshape(-1, orbits, rank_width)


def near_sum(density, sources, near_table):
    running = None
    for column_start in range(0, sources.shape[1], 9):
        picked = jnp.take(density, sources[:, column_start : column_start + 9], axis=1)
        piece_sum = jnp.einsum(
            "olkq,kpq->olp",
            picked,
            near_table[column_start : column_start + 9],
            preferred_element_type=jnp.float32,
        )
        running = piece_sum if running is None else running + piece_sum
    return running


def shifted(values, offset):
    node_count = values.shape[0]
    if abs(offset) >= node_count:
        return jnp.zeros_like(values)
    empty = jnp.zeros((abs(offset), values.shape[1], values.shape[2]), values.dtype)
    if offset > 0:
        return jnp.concatenate([values[offset:], empty], axis=0)
    return jnp.concatenate([empty, values[:offset]], axis=0)


def coarse_couple(moments, coarse_coupling, scale):
    node_count = moments.shape[0]
    odd_rows = (jnp.arange(node_count) % 2).astype(jnp.float32)[:, None, None]
    even_rows = 1.0 - odd_rows

    def apply_matrix(which, offset):
        return jnp.einsum(
            "nos,rs->nor",
            shifted(moments, offset),
            coarse_coupling[which],
            preferred_element_type=jnp.float32,
        )

    running = (
        apply_matrix(1, -2)
        + apply_matrix(2, 2)
        + even_rows * apply_matrix(3, 3)
        + odd_rows * apply_matrix(0, -3)
    )
    return scale * running


def coarse_up(moments, pair_transfer):
    node_count, orbits, rank_width = moments.shape
    shaped = moments.reshape(-1, 2, orbits, rank_width)
    return jnp.einsum(
        "apos,psr->aor", shaped, pair_transfer, preferred_element_type=jnp.float32
    ).astype(jnp.bfloat16)


def coarse_down(coeffs, pair_transfer):
    children = jnp.einsum(
        "aor,psr->apos", coeffs, pair_transfer, preferred_element_type=jnp.float32
    )
    return children.reshape(-1, coeffs.shape[1], coeffs.shape[2])


def coarse_tree(cube_moments, coarse_coupling, pair_transfer):
    levels = [cube_moments]
    while levels[-1].shape[0] > 1:
        levels.append(coarse_up(levels[-1], pair_transfer))
    top_level = len(levels) - 1
    coeffs = coarse_couple(levels[top_level], coarse_coupling, 0.5 ** (3 + top_level)).astype(
        jnp.bfloat16
    )
    for depth_level in range(top_level - 1, -1, -1):
        pushed = coarse_down(coeffs, pair_transfer)
        coupled = coarse_couple(levels[depth_level], coarse_coupling, 0.5 ** (3 + depth_level))
        coeffs = (coupled + pushed).astype(jnp.bfloat16)
    return coeffs


def shards(
    orbitals,
    near_source,
    far_leaf,
    far_mid,
    far_top,
    leaf_basis,
    near_table,
    transfer,
    coupling,
    pair_transfer,
    coarse_coupling,
):
    orbits, leaf_count, points = orbitals.shape
    rank_size = leaf_basis.shape[0]
    device = lax.axis_index("space")
    density = (orbitals * orbitals).astype(jnp.bfloat16)
    layer_size = SIDE * SIDE
    reach_leaves = 12 * layer_size
    density_ext = padded(density, (("space", 1),), layer_size)
    near_start = device * leaf_count - layer_size
    local_moments = leaf_project(density, leaf_basis)
    flattened = local_moments.reshape(leaf_count, orbits * rank_size)
    leaf_ext = padded(flattened, (("space", 0),), reach_leaves).reshape(-1, orbits, rank_size)
    near_field = near_sum(density_ext, near_source - near_start, near_table)
    mid_ext = octant_up(leaf_ext, SIDE, transfer)
    top_ext = octant_up(mid_ext, SIDE // 2, transfer)
    top_count = leaf_count // 64
    mid_count = leaf_count // 8
    top_rim = reach_leaves // 64
    mid_rim = reach_leaves // 8
    top_local = top_ext[top_rim : top_rim + top_count]
    cube_local = octant_up(top_local, SIDE // 4, transfer)
    cube_rows = cube_local.shape[0]
    cube_all = lax.all_gather(
        cube_local.reshape(cube_rows, orbits * rank_size), "space", axis=0, tiled=True
    ).reshape(-1, orbits, rank_size)
    cube_coeffs = coarse_tree(cube_all, coarse_coupling, pair_transfer)
    cube_own = lax.dynamic_slice_in_dim(cube_coeffs, device * cube_rows, cube_rows, 0)
    top_coeffs = (
        couple_rows(top_ext, far_top - (device * top_count - top_rim), coupling, 0.25)
        + octant_down(cube_own, SIDE // 8, transfer)
    ).astype(jnp.bfloat16)
    mid_coeffs = (
        couple_rows(mid_ext, far_mid - (device * mid_count - mid_rim), coupling, 0.5)
        + octant_down(top_coeffs, SIDE // 4, transfer)
    ).astype(jnp.bfloat16)
    leaf_coeffs = (
        couple_rows(leaf_ext, far_leaf - (device * leaf_count - reach_leaves), coupling, 1.0)
        + octant_down(mid_coeffs, SIDE // 2, transfer)
    ).astype(jnp.bfloat16)
    far_field = jnp.einsum(
        "lor,rp->olp", leaf_coeffs, leaf_basis, preferred_element_type=jnp.float32
    )
    potential = near_field + far_field
    hartree = lax.psum(jnp.sum(potential, axis=0).astype(jnp.bfloat16), "orb").astype(jnp.float32)
    return orbitals - relax_step * (hartree[None] - potential) * orbitals


def solution(mesh):
    placed = (
        P("orb", "space", None),
        P("space", None),
        P("space", None),
        P("space", None),
        P("space", None),
        P(),
        P(),
        P(),
        P(),
        P(),
        P(),
    )
    return jax.shard_map(
        shards, mesh=mesh, in_specs=placed, out_specs=P("orb", "space", None), check_vma=False
    )
```

profile of v0, /device:TPU:0, one launch (start us, length us, event | category | flops | bytes accessed | tf_op | source)
XLA Modules:
  0.0 1078.0 jit_solution(17902328975907240493)
XLA Ops:
  15.3 4.8 collective-permute-start
  55.0 9.0 multiply_bitcast_fusion
  77.4 4.4 reshape.258
  105.5 7.3 copy.392
  112.7 71.8 %gather_fusion.2 = bf16[9216,2,256]{2,1,0:T(2,128)(2,1)} fusion(bf16[2,1152,256]{2,0,1:T(2,128)(2,1)S(1)} %copy.392, s32[9216]{0:T(1024)S(1)} %broadcast_clamp_fusion.4), kind=kCustom, calls=%fused_computation.5.clone | custom fusion | bytes 18911232 | tf_op jit(solution)/shard_map/jit(_take)/gather | solution.py:75
  184.6 71.8 %gather_fusion.1 = bf16[9216,2,256]{2,1,0:T(2,128)(2,1)} fusion(bf16[2,1152,256]{2,0,1:T(2,128)(2,1)S(1)} %copy.392, s32[9216]{0:T(1024)S(1)} %broadcast_clamp_fusion.5), kind=kCustom, calls=%fused_computation.4.clone | custom fusion | bytes 18911232 | tf_op jit(solution)/shard_map/jit(_take)/gather | solution.py:75
  256.4 71.8 %gather_fusion = bf16[9216,2,256]{2,1,0:T(2,128)(2,1)} fusion(bf16[2,1152,256]{2,0,1:T(2,128)(2,1)S(1)} %copy.392, s32[9216]{0:T(1024)S(1)} %broadcast_clamp_fusion.6), kind=kCustom, calls=%fused_computation.clone | custom fusion | bytes 18911232 | tf_op jit(solution)/shard_map/jit(_take)/gather | solution.py:75
  328.2 18.5 %fusion.2 = bf16[2,1024,9,256]{3,0,2,1:T(2,128)(2,1)S(1)} fusion(bf16[1024,9,2,256]{3,2,1,0:T(2,128)(2,1)} %bitcast.386, pred[1024,9]{1,0:T(8,128)(4,1)S(1)} %copy-done.18), kind=kLoop, calls=%fused_computation.20 | loop fusion | flops 4718592 | bytes 18883584 | tf_op jit(solution)/shard_map/jit(_take)/select_n | solution.py:75
  350.8 16.6 %fusion.1 = bf16[2,1024,9,256]{3,0,2,1:T(2,128)(2,1)S(1)} fusion(bf16[1024,9,2,256]{3,2,1,0:T(2,128)(2,1)S(1)} %bitcast.385, pred[1024,9]{1,0:T(8,128)(4,1)S(1)} %copy-done.19), kind=kLoop, calls=%fused_computation.19 | loop fusion | flops 4718592 | bytes 18883584 | tf_op jit(solution)/shard_map/jit(_take)/select_n | solution.py:75
  367.5 18.0 %fusion = bf16[2,1024,9,256]{3,0,2,1:T(2,128)(2,1)} fusion(bf16[1024,9,2,256]{3,2,1,0:T(2,128)(2,1)S(1)} %bitcast.382, pred[1024,9]{1,0:T(8,128)(4,1)S(1)} %copy-done.20), kind=kLoop, calls=%fused_computation.18 | loop fusion | flops 4718592 | bytes 18883584 | tf_op jit(solution)/shard_map/jit(_take)/select_n | solution.py:75
  395.6 28.1 %all-gather = bf16[32,2,128]{2,1,0:T(2,128)(2,1)S(1)} all-gather(bf16[1,2,128]{2,1,0:T(2,128)(2,1)S(1)} %reshape.425), channel_id=1, replica_groups=mesh['space'=32,'orb'=4] {'space'}, dimensions={0}, use_global_device_ids=true | all-gather | bytes 16896 | tf_op jit(solution)/shard_map/all_gather | solution.py:182
  449.5 8.2 gather_fusion.10
  463.2 7.1 gather_fusion.9
  475.8 7.1 gather_fusion.8
  488.4 7.1 gather_fusion.7
  504.7 96.4 %gather_fusion.3 = bf16[27648,128]{1,0:T(8,128)(2,1)} fusion(bf16[2560,128]{1,0:T(8,128)(2,1)S(1)} %pad_maximum_fusion.1, s32[27648]{0:T(1024)S(1)} %broadcast_clamp_fusion.3), kind=kCustom, calls=%fused_computation.1.clone | custom fusion | bytes 14266368 | tf_op jit(solution)/shard_map/jit(_take)/gather | solution.py:66
  601.1 11.9 %reshape.448 = bf16[1024,27,128]{2,1,0:T(8,128)(2,1)} reshape(bf16[27648,128]{1,0:T(8,128)(2,1)} %gather_fusion.3) | data formatting | bytes 14155776 | tf_op jit(solution)/shard_map/jit(_take)/gather | solution.py:66
  613.1 15.5 %broadcast_select_fusion.6 = bf16[1024,27,128]{2,1,0:T(8,128)(2,1)S(1)} fusion(bf16[1024,27,128]{2,1,0:T(8,128)(2,1)} %reshape.448, pred[1024,27]{1,0:T(8,128)(4,1)S(1)} %copy-done.17), kind=kLoop, calls=%fused_computation.30 | loop fusion | flops 3538944 | bytes 14183424 | tf_op jit(solution)/shard_map/jit(_take)/select_n | solution.py:66
  632.9 96.4 %gather_fusion.4 = bf16[27648,128]{1,0:T(8,128)(2,1)} fusion(bf16[2560,128]{1,0:T(8,128)(2,1)S(1)} %pad_maximum_fusion.1, s32[27648]{0:T(1024)S(1)} %broadcast_clamp_fusion.2), kind=kCustom, calls=%fused_computation.6.clone | custom fusion | bytes 14266368 | tf_op jit(solution)/shard_map/jit(_take)/gather | solution.py:66
  729.3 11.9 %reshape.452 = bf16[1024,27,128]{2,1,0:T(8,128)(2,1)} reshape(bf16[27648,128]{1,0:T(8,128)(2,1)} %gather_fusion.4) | data formatting | bytes 14155776 | tf_op jit(solution)/shard_map/jit(_take)/gather | solution.py:66
  741.2 96.4 %gather_fusion.5 = bf16[27648,128]{1,0:T(8,128)(2,1)} fusion(bf16[2560,128]{1,0:T(8,128)(2,1)S(1)} %pad_maximum_fusion.1, s32[27648]{0:T(1024)S(1)} %broadcast_clamp_fusion.1), kind=kCustom, calls=%fused_computation.7.clone | custom fusion | bytes 14266368 | tf_op jit(solution)/shard_map/jit(_take)/gather | solution.py:66
  837.6 11.9 %reshape.456 = bf16[1024,27,128]{2,1,0:T(8,128)(2,1)} reshape(bf16[27648,128]{1,0:T(8,128)(2,1)} %gather_fusion.5) | data formatting | bytes 14155776 | tf_op jit(solution)/shard_map/jit(_take)/gather | solution.py:66
  849.5 96.4 %gather_fusion.6 = bf16[27648,128]{1,0:T(8,128)(2,1)} fusion(bf16[2560,128]{1,0:T(8,128)(2,1)S(1)} %pad_maximum_fusion.1, s32[27648]{0:T(1024)S(1)} %copy-done.4), kind=kCustom, calls=%fused_computation.8.clone | custom fusion | bytes 14266368 | tf_op jit(solution)/shard_map/jit(_take)/gather | solution.py:66
  945.9 11.9 %reshape.460 = bf16[1024,27,128]{2,1,0:T(8,128)(2,1)} reshape(bf16[27648,128]{1,0:T(8,128)(2,1)} %gather_fusion.6) | data formatting | bytes 14155776 | tf_op jit(solution)/shard_map/jit(_take)/gather | solution.py:66
  957.9 15.4 %broadcast_select_fusion.5 = bf16[1024,27,128]{2,1,0:T(8,128)(2,1)S(1)} fusion(bf16[1024,27,128]{2,1,0:T(8,128)(2,1)} %reshape.452, pred[1024,27]{1,0:T(8,128)(4,1)S(1)} %copy-done.14), kind=kLoop, calls=%fused_computation.29 | loop fusion | flops 3538944 | bytes 14183424 | tf_op jit(solution)/shard_map/jit(_take)/select_n | solution.py:66
  973.3 4.3 fusion.37
  977.7 15.7 %broadcast_select_fusion.4 = bf16[1024,27,128]{2,1,0:T(8,128)(2,1)S(1)} fusion(bf16[1024,27,128]{2,1,0:T(8,128)(2,1)} %reshape.456, pred[1024,27]{1,0:T(8,128)(4,1)S(1)} %copy-done.15), kind=kLoop, calls=%fused_computation.28 | loop fusion | flops 3538944 | bytes 14183424 | tf_op jit(solution)/shard_map/jit(_take)/select_n | solution.py:66
  993.5 4.3 fusion.34
  997.8 13.7 %broadcast_select_fusion.3 = bf16[1024,27,128]{2,1,0:T(8,128)(2,1)S(1)} fusion(bf16[1024,27,128]{2,1,0:T(8,128)(2,1)S(1)} %bitcast.388, pred[1024,27]{1,0:T(8,128)(4,1)S(1)} %copy-done.16), kind=kLoop, calls=%fused_computation.27 | loop fusion | flops 3538944 | bytes 14183424 | tf_op jit(solution)/shard_map/jit(_take)/select_n | solution.py:66
  1011.6 4.3 fusion.31
  1016.5 7.0 fusion.300
  1023.5 43.0 %all-reduce.22.cloned.1.call-done = bf16[1024,256]{1,0:T(8,128)(2,1)} async-done(((bf16[1024,256]{1,0:T(8,128)(2,1)}), bf16[1024,256]{1,0:T(8,128)(2,1)}) %all-reduce.22.cloned.1.call-update) | async-done | bytes 524304 | tf_op jit(solution)/shard_map/psum | solution.py:203
  (335 shorter events, 154.4 us)
Async XLA Ops:
  6.5 387.6 %copy-start = (bf16[8,64,64]{2,1,0:T(8,128)(2,1)S(1)}, bf16[8,64,64]{2,1,0:T(8,128)(2,1)}, u32[]{:S(2)}) copy-start(bf16[8,64,64]{2,1,0:T(8,128)(2,1)} %param.26) | copy-start | bytes 196612
  6.5 29.9 %copy-start.11 = (bf16[4,64,64]{2,1,0:T(8,128)(2,1)S(1)}, bf16[4,64,64]{2,1,0:T(8,128)(2,1)}, u32[]{:S(2)}) copy-start(bf16[4,64,64]{2,1,0:T(8,128)(2,1)} %param.29) | copy-start | bytes 98308
  6.5 25.2 %copy-start.24 = (s32[1024,108]{0,1:T(8,128)S(1)}, s32[1024,108]{0,1:T(8,128)}, u32[]{:S(2)}) copy-start(s32[1024,108]{0,1:T(8,128)} %param.21) | copy-start | bytes 1327108
  6.5 30.7 %copy-start.9 = (bf16[2,64,64]{2,1,0:T(8,128)(2,1)S(1)}, bf16[2,64,64]{2,1,0:T(8,128)(2,1)}, u32[]{:S(2)}) copy-start(bf16[2,64,64]{2,1,0:T(8,128)(2,1)} %param.28) | copy-start | bytes 49156
  6.5 34.3 %copy-start.2 = (bf16[108,64,64]{0,2,1:T(8,128)(2,1)S(1)}, bf16[108,64,64]{0,2,1:T(8,128)(2,1)}, u32[]{:S(2)}) copy-start(bf16[108,64,64]{0,2,1:T(8,128)(2,1)} %param.27) | copy-start | bytes 2654212
  6.5 1059.9 %all-reduce.22.cloned.1.call-start = ((), (), s32[]{:S(2)}) async-start(), calls=%async_computation | async-start | bytes 1048576 | tf_op jit(solution)/shard_map/psum | solution.py:203
  10.5 379.0 %collective-permute-start.2 = (bf16[768,128]{1,0:T(8,128)(2,1)}, bf16[768,128]{1,0:T(8,128)(2,1)}, u32[]{:S(2)}, u32[]{:S(2)}) collective-permute-start(bf16[768,128]{1,0:T(8,128)(2,1)} %copy.403), channel_id=1, source_target_pairs={{0,4},{4,8},{8,12},{12,16},{16,20},{20,24},{24,28},{28,32},{32,36}... | collective-permute-start | bytes 589832 | tf_op jit(solution)/shard_map/ppermute | solution.py:18
  13.3 376.3 %collective-permute-start.3 = (bf16[768,128]{1,0:T(8,128)(2,1)}, bf16[768,128]{1,0:T(8,128)(2,1)}, u32[]{:S(2)}, u32[]{:S(2)}) collective-permute-start(bf16[768,128]{1,0:T(8,128)(2,1)} %copy.404), channel_id=1, source_target_pairs={{4,0},{8,4},{12,8},{16,12},{20,16},{24,20},{28,24},{32,28},{36,32}... | collective-permute-start | bytes 589832 | tf_op jit(solution)/shard_map/ppermute | solution.py:20
  15.3 89.3 %collective-permute-start = (bf16[2,64,256]{2,1,0:T(8,128)(2,1)}, bf16[2,64,256]{2,1,0:T(8,128)(2,1)}, u32[]{:S(2)}, u32[]{:S(2)}) collective-permute-start(bf16[2,64,256]{2,1,0:T(8,128)(2,1)} %get-tuple-element.6), channel_id=1, source_target_pairs={{0,4},{4,8},{8,12},{12,16},{16,20},{20,24},{24,28},{28,32},{32,36}... | collective-permute-start | bytes 196616 | tf_op jit(solution)/shard_map/ppermute | solution.py:18
  20.1 84.4 %collective-permute-start.1 = (bf16[2,64,256]{2,1,0:T(8,128)(2,1)}, bf16[2,64,256]{2,1,0:T(8,128)(2,1)}, u32[]{:S(2)}, u32[]{:S(2)}) collective-permute-start(bf16[2,64,256]{2,1,0:T(8,128)(2,1)} %get-tuple-element.8), channel_id=1, source_target_pairs={{4,0},{8,4},{12,8},{16,12},{20,16},{24,20},{28,24},{32,28},{36,32}... | collective-permute-start | bytes 196616 | tf_op jit(solution)/shard_map/ppermute | solution.py:20
  64.0 19.5 %copy-start.35 = (s32[128,27]{0,1:T(8,128)S(1)}, s32[128,27]{0,1:T(8,128)}, u32[]{:S(2)}) copy-start(s32[128,27]{0,1:T(8,128)} %get-tuple-element.37) | copy-start | bytes 41476
  64.0 20.4 %copy-start.41 = (pred[128,27]{0,1:T(8,128)(4,1)S(1)}, pred[128,27]{0,1:T(8,128)(4,1)}, u32[]{:S(2)}) copy-start(pred[128,27]{0,1:T(8,128)(4,1)} %get-tuple-element.33) | copy-start | bytes 10372
  64.0 25.9 %copy-start.23 = (s32[1024,27]{0,1:T(8,128)S(1)}, s32[1024,27]{0,1:T(8,128)}, u32[]{:S(2)}) copy-start(s32[1024,27]{0,1:T(8,128)} %get-tuple-element.21) | copy-start | bytes 331780
  64.0 27.3 %copy-start.22 = (s32[1024,27]{0,1:T(8,128)S(1)}, s32[1024,27]{0,1:T(8,128)}, u32[]{:S(2)}) copy-start(s32[1024,27]{0,1:T(8,128)} %get-tuple-element.20) | copy-start | bytes 331780
  67.5 26.1 %copy-start.21 = (s32[1024,27]{0,1:T(8,128)S(1)}, s32[1024,27]{0,1:T(8,128)}, u32[]{:S(2)}) copy-start(s32[1024,27]{0,1:T(8,128)} %get-tuple-element.19) | copy-start | bytes 331780
  73.2 26.3 %copy-start.29 = (s32[1024,9]{0,1:T(8,128)S(1)}, s32[1024,9]{0,1:T(8,128)}, u32[]{:S(2)}) copy-start(s32[1024,9]{0,1:T(8,128)} %get-tuple-element.30) | copy-start | bytes 110596
  77.4 24.3 %copy-start.28 = (s32[1024,9]{0,1:T(8,128)S(1)}, s32[1024,9]{0,1:T(8,128)}, u32[]{:S(2)}) copy-start(s32[1024,9]{0,1:T(8,128)} %get-tuple-element.28) | copy-start | bytes 110596
  256.4 71.8 %copy-start.18 = (pred[1024,9]{1,0:T(8,128)(4,1)S(1)}, pred[1024,9]{1,0:T(8,128)(4,1)}, u32[]{:S(2)}) copy-start(pred[1024,9]{1,0:T(8,128)(4,1)} %copy.398) | copy-start | bytes 27652
  328.2 22.5 %slice-start.3 = ((s8[9437184]{0:T(1024)(128)(4,1)}), s8[4194304]{0:T(1024)(128)(4,1)S(1)}, s32[]{:S(2)}) async-start(s8[9437184]{0:T(1024)(128)(4,1)} %bitcast.383), calls=%async_computation.4 | async-start | bytes 8388608
  328.2 22.5 %slice-start.4 = ((s8[9437184]{0:T(1024)(128)(4,1)}), s8[4194304]{0:T(1024)(128)(4,1)S(1)}, s32[]{:S(2)}) async-start(s8[9437184]{0:T(1024)(128)(4,1)} %bitcast.383), calls=%async_computation.5 | async-start | bytes 8388608
  346.7 20.7 %slice-start = ((s8[9437184]{0:T(1024)(128)(4,1)}), s8[4194304]{0:T(1024)(128)(4,1)S(1)}, s32[]{:S(2)}) async-start(s8[9437184]{0:T(1024)(128)(4,1)} %bitcast.380), calls=%async_computation.1 | async-start | bytes 8388608
  346.7 20.7 %slice-start.1 = ((s8[9437184]{0:T(1024)(128)(4,1)}), s8[1048576]{0:T(1024)(128)(4,1)S(1)}, s32[]{:S(2)}) async-start(s8[9437184]{0:T(1024)(128)(4,1)} %bitcast.380), calls=%async_computation.2 | async-start | bytes 2097152
  389.5 34.2 %copy-start.10 = (bf16[2,64,64]{2,1,0:T(8,128)(2,1)S(1)}, bf16[2,64,64]{2,1,0:T(8,128)(2,1)}, u32[]{:S(2)}) copy-start(bf16[2,64,64]{2,1,0:T(8,128)(2,1)} %param.28) | copy-start | bytes 49156
  389.5 35.2 %copy-start.12 = (bf16[4,64,64]{2,1,0:T(8,128)(2,1)S(1)}, bf16[4,64,64]{2,1,0:T(8,128)(2,1)}, u32[]{:S(2)}) copy-start(bf16[4,64,64]{2,1,0:T(8,128)(2,1)} %param.29) | copy-start | bytes 98308
  389.5 47.4 %copy-start.37 = (s32[1024]{0:T(1024)S(1)}, s32[1024]{0:T(1024)}, u32[]{:S(2)}) copy-start(s32[1024]{0:T(1024)} %pad_clamp_fusion.7) | copy-start | bytes 12292
  389.5 49.0 %copy-start.38 = (s32[1024]{0:T(1024)S(1)}, s32[1024]{0:T(1024)}, u32[]{:S(2)}) copy-start(s32[1024]{0:T(1024)} %pad_clamp_fusion.6) | copy-start | bytes 12292
  389.6 51.2 %copy-start.39 = (s32[1024]{0:T(1024)S(1)}, s32[1024]{0:T(1024)}, u32[]{:S(2)}) copy-start(s32[1024]{0:T(1024)} %pad_clamp_fusion.5) | copy-start | bytes 12292
  394.7 54.3 %copy-start.6 = (bf16[27,128,128]{2,1,0:T(8,128)(2,1)S(1)}, bf16[27,128,128]{2,1,0:T(8,128)(2,1)}, u32[]{:S(2)}) copy-start(bf16[27,128,128]{2,1,0:T(8,128)(2,1)} %reshape.258) | copy-start | bytes 2654212
  973.3 24.5 %slice-start.6 = ((s8[8388608]{0:T(1024)(128)(4,1)}), s8[4194304]{0:T(1024)(128)(4,1)S(1)}, s32[]{:S(2)}) async-start(s8[8388608]{0:T(1024)(128)(4,1)} %bitcast.387), calls=%async_computation.7 | async-start | bytes 8388608
  977.7 20.1 %slice-start.7 = ((s8[8388608]{0:T(1024)(128)(4,1)}), s8[4194304]{0:T(1024)(128)(4,1)S(1)}, s32[]{:S(2)}) async-start(s8[8388608]{0:T(1024)(128)(4,1)} %bitcast.387), calls=%async_computation.8 | async-start | bytes 8388608
  1016.5 51.1 %copy-start.3 = (f32[2,1024,256]{2,1,0:T(8,128)S(1)}, f32[2,1024,256]{2,1,0:T(8,128)}, u32[]{:S(2)}) copy-start(f32[2,1024,256]{2,1,0:T(8,128)} %param.19) | copy-start | bytes 6291460
  1016.5 54.3 %copy-start.1 = (bf16[8,64,64]{2,1,0:T(8,128)(2,1)S(1)}, bf16[8,64,64]{2,1,0:T(8,128)(2,1)}, u32[]{:S(2)}) copy-start(bf16[8,64,64]{2,1,0:T(8,128)(2,1)} %param.26) | copy-start | bytes 196612
  (31 other events, 372.2 us)
Sparse Core Ops, SparseCore 0:
  1023.6 42.8 all-reduce.21
where the time goes:
time: 1090 us; the launch traced here: 1080 us
  local copies, waits for them, and re-layouts  761 us (70%)
  other arithmetic  162 us (15%)
  matrix products  58.8 us (5%)
  waiting for transfers between devices  43 us (4%)
  blocking collectives  28.1 us (3%)
  between operations  15 us (1%)
    gather x24, local copies, waits for them, and re-layouts, couple_rows(): jnp.take(flattened, sources[:, column_start:column_start + 27], axis=0)  475 us
    gather x3, local copies, waits for them, and re-layouts, near_sum(): jnp.take(density, sources[:, column_start:column_start + 9], axis=1)  215 us
    select_n x13, other arithmetic, couple_rows(): jnp.take(flattened, sources[:, column_start:column_start + 27], axis=0)  74.5 us
    select_n x4, other arithmetic, near_sum(): jnp.take(density, sources[:, column_start:column_start + 9], axis=1)  53.8 us
    psum x1, waiting for transfers between devices, shards(): lax.psum(jnp.sum(potential, axis=0).astype(jnp.bfloat16), 'orb')  43 us
    all_gather x1, blocking collectives, shards(): lax.all_gather(cube_local.reshape(cube_rows, orbits * rank_size), 'space'...  28.1 us
    dot_general x12, matrix products, couple_rows(): jnp.einsum('lkx,kxy->ly', picked, widened, preferred_element_type=jnp.flo...  26 us
  transfers between devices with their start and end apart: 5, of which 1 were waited for; matrix products, arithmetic and copies ran while one was open for 34% of the time, Pallas kernels for 0%

commit v1 on v0

--- a/solution.py
+++ b/solution.py
@@ -179,8 +179,14 @@
     top_local = top_ext[top_rim : top_rim + top_count]
     cube_local = octant_up(top_local, SIDE // 4, transfer)
     cube_rows = cube_local.shape[0]
-    cube_all = lax.all_gather(
-        cube_local.reshape(cube_rows, orbits * rank_size), "space", axis=0, tiled=True
+    cube_all = jnp.concatenate(
+        lax.all_to_all(
+            jnp.stack([cube_local.reshape(cube_rows, orbits * rank_size)] * lax.axis_size("space")),
+            "space",
+            0,
+            0,
+        ),
+        axis=0,
     ).reshape(-1, orbits, rank_size)
     cube_coeffs = coarse_tree(cube_all, coarse_coupling, pair_transfer)
     cube_own = lax.dynamic_slice_in_dim(cube_coeffs, device * cube_rows, cube_rows, 0)

time: 1090 us -> 1050 us (0.963)
  blocking collectives: 28.1 us -> 0 us
  other arithmetic: 162 us -> 150 us
  starting transfers between devices: 9.42 us -> 21.3 us
    all_gather x1 -> x0, blocking collectives: 28.1 us -> none  [shards(): lax.all_gather(cube_local.reshape(cube_rows, orbits * rank_size), 'space'...]
    all_to_all x0 -> x1, starting transfers between devices: none -> 11.9 us  [shards(): lax.all_to_all(jnp.stack([cube_local.reshape(cube_rows, orbits * rank_siz...]
    select_n x13, other arithmetic: 74.5 us -> 63.2 us  [couple_rows(): jnp.take(flattened, sources[:, column_start:column_start + 27], axis=0)]
  transfers between devices with their start and end apart: 5 -> 6, of which waited for: 1 -> 1; matrix products, arithmetic and copies ran while one was open for 34% -> 89% of each run, Pallas kernels for 0% -> 0%
where the time goes in v1:
time: 1050 us
  local copies, waits for them, and re-layouts  760 us (72%)
  other arithmetic  150 us (14%)
  matrix products  54.6 us (5%)
  waiting for transfers between devices  44.4 us (4%)
  starting transfers between devices  21.3 us (2%)
  between operations  15.3 us (1%)
    gather x24, local copies, waits for them, and re-layouts, couple_rows(): jnp.take(flattened, sources[:, column_start:column_start + 27], axis=0)  475 us
    gather x3, local copies, waits for them, and re-layouts, near_sum(): jnp.take(density, sources[:, column_start:column_start + 9], axis=1)  215 us
    select_n x13, other arithmetic, couple_rows(): jnp.take(flattened, sources[:, column_start:column_start + 27], axis=0)  63.2 us
    select_n x4, other arithmetic, near_sum(): jnp.take(density, sources[:, column_start:column_start + 9], axis=1)  53.4 us
    psum x1, waiting for transfers between devices, shards(): lax.psum(jnp.sum(potential, axis=0).astype(jnp.bfloat16), 'orb')  44.4 us
    dot_general x12, matrix products, couple_rows(): jnp.einsum('lkx,kxy->ly', picked, widened, preferred_element_type=jnp.flo...  25.9 us
  transfers between devices with their start and end apart: 6, of which 1 were waited for; matrix products, arithmetic and copies ran while one was open for 89% of the time, Pallas kernels for 0%

profile of v1, /device:TPU:0, one launch (start us, length us, event | category | flops | bytes accessed | tf_op | source)
XLA Modules:
  0.0 1045.7 jit_solution(13487662152618142036)
XLA Ops:
  15.2 4.9 collective-permute-start
  54.8 9.0 multiply_bitcast_fusion
  77.2 4.4 reshape.256
  103.7 7.3 copy.305
  111.0 71.8 %gather_fusion.2 = bf16[9216,2,256]{2,1,0:T(2,128)(2,1)} fusion(bf16[2,1152,256]{2,0,1:T(2,128)(2,1)S(1)} %copy.305, s32[9216]{0:T(1024)S(1)} %broadcast_clamp_fusion.4), kind=kCustom, calls=%fused_computation.5.clone | custom fusion | bytes 18911232 | tf_op jit(solution)/shard_map/jit(_take)/gather | solution.py:75
  182.8 71.9 %gather_fusion.1 = bf16[9216,2,256]{2,1,0:T(2,128)(2,1)} fusion(bf16[2,1152,256]{2,0,1:T(2,128)(2,1)S(1)} %copy.305, s32[9216]{0:T(1024)S(1)} %broadcast_clamp_fusion.5), kind=kCustom, calls=%fused_computation.4.clone | custom fusion | bytes 18911232 | tf_op jit(solution)/shard_map/jit(_take)/gather | solution.py:75
  254.6 71.8 %gather_fusion = bf16[9216,2,256]{2,1,0:T(2,128)(2,1)} fusion(bf16[2,1152,256]{2,0,1:T(2,128)(2,1)S(1)} %copy.305, s32[9216]{0:T(1024)S(1)} %broadcast_clamp_fusion.6), kind=kCustom, calls=%fused_computation.clone | custom fusion | bytes 18911232 | tf_op jit(solution)/shard_map/jit(_take)/gather | solution.py:75
  326.5 18.5 %fusion.2 = bf16[2,1024,9,256]{3,0,2,1:T(2,128)(2,1)S(1)} fusion(bf16[1024,9,2,256]{3,2,1,0:T(2,128)(2,1)} %bitcast.385, pred[1024,9]{1,0:T(8,128)(4,1)S(1)} %copy-done.22), kind=kLoop, calls=%fused_computation.20 | loop fusion | flops 4718592 | bytes 18883584 | tf_op jit(solution)/shard_map/jit(_take)/select_n | solution.py:75
  349.0 16.6 %fusion.1 = bf16[2,1024,9,256]{3,0,2,1:T(2,128)(2,1)S(1)} fusion(bf16[1024,9,2,256]{3,2,1,0:T(2,128)(2,1)S(1)} %bitcast.384, pred[1024,9]{1,0:T(8,128)(4,1)S(1)} %copy-done.23), kind=kLoop, calls=%fused_computation.19 | loop fusion | flops 4718592 | bytes 18883584 | tf_op jit(solution)/shard_map/jit(_take)/select_n | solution.py:75
  365.7 17.7 %fusion = bf16[2,1024,9,256]{3,0,2,1:T(2,128)(2,1)} fusion(bf16[1024,9,2,256]{3,2,1,0:T(2,128)(2,1)S(1)} %bitcast.381, pred[1024,9]{1,0:T(8,128)(4,1)S(1)} %copy-done.24), kind=kLoop, calls=%fused_computation.18 | loop fusion | flops 4718592 | bytes 18883584 | tf_op jit(solution)/shard_map/jit(_take)/select_n | solution.py:75
  394.0 11.9 %all-to-all-start = ((bf16[32,2,128]{2,1,0:T(2,128)(2,1)}), bf16[32,2,128]{2,1,0:T(2,128)(2,1)}, u32[]{:S(2)}, u32[]{:S(2)}) async-start(bf16[32,2,128]{2,1,0:T(2,128)(2,1)} %stack.3), calls=%async_computation | async-start | bytes 32768 | tf_op jit(solution)/shard_map/all_to_all | solution.py:183
  414.3 7.1 gather_fusion.10
  422.7 7.1 gather_fusion.9
  431.1 7.1 gather_fusion.8
  439.6 7.1 gather_fusion.7
  448.0 96.4 %gather_fusion.3 = bf16[27648,128]{1,0:T(8,128)(2,1)} fusion(bf16[2560,128]{1,0:T(8,128)(2,1)S(1)} %pad_maximum_fusion.1, s32[27648]{0:T(1024)S(1)} %broadcast_clamp_fusion.3), kind=kCustom, calls=%fused_computation.1.clone | custom fusion | bytes 14266368 | tf_op jit(solution)/shard_map/jit(_take)/gather | solution.py:66
  544.4 11.9 %reshape.438 = bf16[1024,27,128]{2,1,0:T(8,128)(2,1)} reshape(bf16[27648,128]{1,0:T(8,128)(2,1)} %gather_fusion.3) | data formatting | bytes 14155776 | tf_op jit(solution)/shard_map/jit(_take)/gather | solution.py:66
  557.4 15.4 %broadcast_select_fusion.6 = bf16[1024,27,128]{2,1,0:T(8,128)(2,1)S(1)} fusion(bf16[1024,27,128]{2,1,0:T(8,128)(2,1)} %reshape.438, pred[1024,27]{1,0:T(8,128)(4,1)S(1)} %copy-done.21), kind=kLoop, calls=%fused_computation.30 | loop fusion | flops 3538944 | bytes 14183424 | tf_op jit(solution)/shard_map/jit(_take)/select_n | solution.py:66
  572.8 5.1 fusion.19
  577.9 96.4 %gather_fusion.4 = bf16[27648,128]{1,0:T(8,128)(2,1)} fusion(bf16[2560,128]{1,0:T(8,128)(2,1)S(1)} %pad_maximum_fusion.1, s32[27648]{0:T(1024)S(1)} %broadcast_clamp_fusion.2), kind=kCustom, calls=%fused_computation.6.clone | custom fusion | bytes 14266368 | tf_op jit(solution)/shard_map/jit(_take)/gather | solution.py:66
  674.3 11.9 %reshape.442 = bf16[1024,27,128]{2,1,0:T(8,128)(2,1)} reshape(bf16[27648,128]{1,0:T(8,128)(2,1)} %gather_fusion.4) | data formatting | bytes 14155776 | tf_op jit(solution)/shard_map/jit(_take)/gather | solution.py:66
  686.2 96.4 %gather_fusion.5 = bf16[27648,128]{1,0:T(8,128)(2,1)} fusion(bf16[2560,128]{1,0:T(8,128)(2,1)S(1)} %pad_maximum_fusion.1, s32[27648]{0:T(1024)S(1)} %broadcast_clamp_fusion.1), kind=kCustom, calls=%fused_computation.7.clone | custom fusion | bytes 14266368 | tf_op jit(solution)/shard_map/jit(_take)/gather | solution.py:66
  782.6 11.9 %reshape.446 = bf16[1024,27,128]{2,1,0:T(8,128)(2,1)} reshape(bf16[27648,128]{1,0:T(8,128)(2,1)} %gather_fusion.5) | data formatting | bytes 14155776 | tf_op jit(solution)/shard_map/jit(_take)/gather | solution.py:66
  794.6 96.4 %gather_fusion.6 = bf16[27648,128]{1,0:T(8,128)(2,1)} fusion(bf16[2560,128]{1,0:T(8,128)(2,1)S(1)} %pad_maximum_fusion.1, s32[27648]{0:T(1024)S(1)} %copy-done.7), kind=kCustom, calls=%fused_computation.8.clone | custom fusion | bytes 14266368 | tf_op jit(solution)/shard_map/jit(_take)/gather | solution.py:66
  891.0 12.2 %reshape.450 = bf16[1024,27,128]{2,1,0:T(8,128)(2,1)} reshape(bf16[27648,128]{1,0:T(8,128)(2,1)} %gather_fusion.6) | data formatting | bytes 14155776 | tf_op jit(solution)/shard_map/jit(_take)/gather | solution.py:66
  913.2 13.7 %broadcast_select_fusion.5 = bf16[1024,27,128]{2,1,0:T(8,128)(2,1)S(1)} fusion(bf16[1024,27,128]{2,1,0:T(8,128)(2,1)S(1)} %bitcast.391, pred[1024,27]{1,0:T(8,128)(4,1)S(1)} %copy-done.18), kind=kLoop, calls=%fused_computation.29 | loop fusion | flops 3538944 | bytes 14183424 | tf_op jit(solution)/shard_map/jit(_take)/select_n | solution.py:66
  927.0 4.3 fusion.37
  931.4 13.7 %broadcast_select_fusion.4 = bf16[1024,27,128]{2,1,0:T(8,128)(2,1)S(1)} fusion(bf16[1024,27,128]{2,1,0:T(8,128)(2,1)S(1)} %bitcast.389, pred[1024,27]{1,0:T(8,128)(4,1)S(1)} %copy-done.19), kind=kLoop, calls=%fused_computation.28 | loop fusion | flops 3538944 | bytes 14183424 | tf_op jit(solution)/shard_map/jit(_take)/select_n | solution.py:66
  945.2 5.1 fusion.34
  950.3 14.0 %broadcast_select_fusion.3 = bf16[1024,27,128]{2,1,0:T(8,128)(2,1)S(1)} fusion(bf16[1024,27,128]{2,1,0:T(8,128)(2,1)S(1)} %bitcast.387, pred[1024,27]{1,0:T(8,128)(4,1)S(1)} %copy-done.20), kind=kLoop, calls=%fused_computation.27 | loop fusion | flops 3538944 | bytes 14183424 | tf_op jit(solution)/shard_map/jit(_take)/select_n | solution.py:66
  979.1 10.7 %fusion.300 = (bf16[1024,256]{1,0:T(8,128)(2,1)}, f32[2,1024,256]{2,1,0:T(8,128)}) fusion(f32[1024,2,256]{2,0,1:T(8,128)S(1)} %fusion.103, f32[2,1024,256,1]{2,1,3,0:T(8,128)} %fusion.3, f32[2,1024,256,1]{2,1,3,0:T(8,128)} %fusion.5, bf16[27,256,256]{2,1,0:T(8,128)(2,1)} %param.25, bf16[2,1024,9,256]{3,0,2,1:T(2,128)(2,1)} %fusion), kind=kOutput, calls=%fused_computation.419 | convolution fusion | flops 2417754112 | bytes 19529728 | tf_op jit(solution)/shard_map/olkq,kpq->olp/dot_general | solution.py:76
  989.8 44.4 %all-reduce.22.cloned.1.call-done = bf16[1024,256]{1,0:T(8,128)(2,1)} async-done(((bf16[1024,256]{1,0:T(8,128)(2,1)}), bf16[1024,256]{1,0:T(8,128)(2,1)}) %all-reduce.22.cloned.1.call-update) | async-done | bytes 524304 | tf_op jit(solution)/shard_map/psum | solution.py:209
  (395 shorter events, 136.1 us)
Async XLA Ops:
  6.5 385.5 %copy-start = (bf16[8,64,64]{2,1,0:T(8,128)(2,1)S(1)}, bf16[8,64,64]{2,1,0:T(8,128)(2,1)}, u32[]{:S(2)}) copy-start(bf16[8,64,64]{2,1,0:T(8,128)(2,1)} %param.26) | copy-start | bytes 196612
  6.5 29.7 %copy-start.15 = (bf16[4,64,64]{2,1,0:T(8,128)(2,1)S(1)}, bf16[4,64,64]{2,1,0:T(8,128)(2,1)}, u32[]{:S(2)}) copy-start(bf16[4,64,64]{2,1,0:T(8,128)(2,1)} %param.29) | copy-start | bytes 98308
  6.5 24.9 %copy-start.29 = (s32[1024,108]{0,1:T(8,128)S(1)}, s32[1024,108]{0,1:T(8,128)}, u32[]{:S(2)}) copy-start(s32[1024,108]{0,1:T(8,128)} %param.21) | copy-start | bytes 1327108
  6.5 30.5 %copy-start.13 = (bf16[2,64,64]{2,1,0:T(8,128)(2,1)S(1)}, bf16[2,64,64]{2,1,0:T(8,128)(2,1)}, u32[]{:S(2)}) copy-start(bf16[2,64,64]{2,1,0:T(8,128)(2,1)} %param.28) | copy-start | bytes 49156
  6.5 34.1 %copy-start.1 = (bf16[108,64,64]{0,2,1:T(8,128)(2,1)S(1)}, bf16[108,64,64]{0,2,1:T(8,128)(2,1)}, u32[]{:S(2)}) copy-start(bf16[108,64,64]{0,2,1:T(8,128)(2,1)} %param.27) | copy-start | bytes 2654212
  10.5 376.9 %collective-permute-start.2 = (bf16[768,128]{1,0:T(8,128)(2,1)}, bf16[768,128]{1,0:T(8,128)(2,1)}, u32[]{:S(2)}, u32[]{:S(2)}) collective-permute-start(bf16[768,128]{1,0:T(8,128)(2,1)} %copy.316), channel_id=1, source_target_pairs={{0,4},{4,8},{8,12},{12,16},{16,20},{20,24},{24,28},{28,32},{32,36}... | collective-permute-start | bytes 589832 | tf_op jit(solution)/shard_map/ppermute | solution.py:18
  13.2 374.1 %collective-permute-start.3 = (bf16[768,128]{1,0:T(8,128)(2,1)}, bf16[768,128]{1,0:T(8,128)(2,1)}, u32[]{:S(2)}, u32[]{:S(2)}) collective-permute-start(bf16[768,128]{1,0:T(8,128)(2,1)} %copy.317), channel_id=1, source_target_pairs={{4,0},{8,4},{12,8},{16,12},{20,16},{24,20},{28,24},{32,28},{36,32}... | collective-permute-start | bytes 589832 | tf_op jit(solution)/shard_map/ppermute | solution.py:20
  15.2 87.5 %collective-permute-start = (bf16[2,64,256]{2,1,0:T(8,128)(2,1)}, bf16[2,64,256]{2,1,0:T(8,128)(2,1)}, u32[]{:S(2)}, u32[]{:S(2)}) collective-permute-start(bf16[2,64,256]{2,1,0:T(8,128)(2,1)} %get-tuple-element.6), channel_id=1, source_target_pairs={{0,4},{4,8},{8,12},{12,16},{16,20},{20,24},{24,28},{28,32},{32,36}... | collective-permute-start | bytes 196616 | tf_op jit(solution)/shard_map/ppermute | solution.py:18
  20.1 82.7 %collective-permute-start.1 = (bf16[2,64,256]{2,1,0:T(8,128)(2,1)}, bf16[2,64,256]{2,1,0:T(8,128)(2,1)}, u32[]{:S(2)}, u32[]{:S(2)}) collective-permute-start(bf16[2,64,256]{2,1,0:T(8,128)(2,1)} %get-tuple-element.8), channel_id=1, source_target_pairs={{4,0},{8,4},{12,8},{16,12},{20,16},{24,20},{28,24},{32,28},{36,32}... | collective-permute-start | bytes 196616 | tf_op jit(solution)/shard_map/ppermute | solution.py:20
  63.8 20.4 %copy-start.55 = (pred[128,27]{0,1:T(8,128)(4,1)S(1)}, pred[128,27]{0,1:T(8,128)(4,1)}, u32[]{:S(2)}) copy-start(pred[128,27]{0,1:T(8,128)(4,1)} %get-tuple-element.33) | copy-start | bytes 10372
  63.8 21.1 %copy-start.46 = (s32[128,27]{0,1:T(8,128)S(1)}, s32[128,27]{0,1:T(8,128)}, u32[]{:S(2)}) copy-start(s32[128,27]{0,1:T(8,128)} %get-tuple-element.38) | copy-start | bytes 41476
  63.8 22.1 %copy-start.54 = (pred[128,27]{0,1:T(8,128)(4,1)S(1)}, pred[128,27]{0,1:T(8,128)(4,1)}, u32[]{:S(2)}) copy-start(pred[128,27]{0,1:T(8,128)(4,1)} %get-tuple-element.34) | copy-start | bytes 10372
  63.8 23.7 %copy-start.53 = (pred[128,27]{0,1:T(8,128)(4,1)S(1)}, pred[128,27]{0,1:T(8,128)(4,1)}, u32[]{:S(2)}) copy-start(pred[128,27]{0,1:T(8,128)(4,1)} %get-tuple-element.31) | copy-start | bytes 10372
  63.8 25.0 %copy-start.41 = (pred[1024,27]{0,1:T(8,128)(4,1)S(1)}, pred[1024,27]{0,1:T(8,128)(4,1)}, u32[]{:S(2)}) copy-start(pred[1024,27]{0,1:T(8,128)(4,1)} %get-tuple-element.18) | copy-start | bytes 82948
  63.8 28.1 %copy-start.26 = (s32[1024,27]{0,1:T(8,128)S(1)}, s32[1024,27]{0,1:T(8,128)}, u32[]{:S(2)}) copy-start(s32[1024,27]{0,1:T(8,128)} %get-tuple-element.20) | copy-start | bytes 331780
  67.3 25.2 %copy-start.40 = (pred[1024,27]{0,1:T(8,128)(4,1)S(1)}, pred[1024,27]{0,1:T(8,128)(4,1)}, u32[]{:S(2)}) copy-start(pred[1024,27]{0,1:T(8,128)(4,1)} %get-tuple-element.16) | copy-start | bytes 82948
  67.3 26.1 %copy-start.25 = (s32[1024,27]{0,1:T(8,128)S(1)}, s32[1024,27]{0,1:T(8,128)}, u32[]{:S(2)}) copy-start(s32[1024,27]{0,1:T(8,128)} %get-tuple-element.19) | copy-start | bytes 331780
  67.3 27.3 %copy-start.39 = (pred[1024,27]{0,1:T(8,128)(4,1)S(1)}, pred[1024,27]{0,1:T(8,128)(4,1)}, u32[]{:S(2)}) copy-start(pred[1024,27]{0,1:T(8,128)(4,1)} %get-tuple-element.15) | copy-start | bytes 82948
  71.6 23.9 %copy-start.37 = (s32[1024,9]{0,1:T(8,128)S(1)}, s32[1024,9]{0,1:T(8,128)}, u32[]{:S(2)}) copy-start(s32[1024,9]{0,1:T(8,128)} %get-tuple-element.29) | copy-start | bytes 110596
  73.0 24.8 %copy-start.36 = (s32[1024,9]{0,1:T(8,128)S(1)}, s32[1024,9]{0,1:T(8,128)}, u32[]{:S(2)}) copy-start(s32[1024,9]{0,1:T(8,128)} %get-tuple-element.30) | copy-start | bytes 110596
  77.2 22.7 %copy-start.35 = (s32[1024,9]{0,1:T(8,128)S(1)}, s32[1024,9]{0,1:T(8,128)}, u32[]{:S(2)}) copy-start(s32[1024,9]{0,1:T(8,128)} %get-tuple-element.28) | copy-start | bytes 110596
  254.6 71.8 %copy-start.22 = (pred[1024,9]{1,0:T(8,128)(4,1)S(1)}, pred[1024,9]{1,0:T(8,128)(4,1)}, u32[]{:S(2)}) copy-start(pred[1024,9]{1,0:T(8,128)(4,1)} %copy.311) | copy-start | bytes 27652
  326.5 22.5 %slice-start.3 = ((s8[9437184]{0:T(1024)(128)(4,1)}), s8[4194304]{0:T(1024)(128)(4,1)S(1)}, s32[]{:S(2)}) async-start(s8[9437184]{0:T(1024)(128)(4,1)} %bitcast.382), calls=%async_computation.5 | async-start | bytes 8388608
  326.5 22.5 %slice-start.4 = ((s8[9437184]{0:T(1024)(128)(4,1)}), s8[4194304]{0:T(1024)(128)(4,1)S(1)}, s32[]{:S(2)}) async-start(s8[9437184]{0:T(1024)(128)(4,1)} %bitcast.382), calls=%async_computation.6 | async-start | bytes 8388608
  345.0 20.7 %slice-start = ((s8[9437184]{0:T(1024)(128)(4,1)}), s8[4194304]{0:T(1024)(128)(4,1)S(1)}, s32[]{:S(2)}) async-start(s8[9437184]{0:T(1024)(128)(4,1)} %bitcast.379), calls=%async_computation.2 | async-start | bytes 8388608
  345.0 20.7 %slice-start.1 = ((s8[9437184]{0:T(1024)(128)(4,1)}), s8[1048576]{0:T(1024)(128)(4,1)S(1)}, s32[]{:S(2)}) async-start(s8[9437184]{0:T(1024)(128)(4,1)} %bitcast.379), calls=%async_computation.3 | async-start | bytes 2097152
  387.4 20.6 %copy-start.50 = (s32[1024]{0:T(1024)S(1)}, s32[1024]{0:T(1024)}, u32[]{:S(2)}) copy-start(s32[1024]{0:T(1024)} %pad_clamp_fusion.6) | copy-start | bytes 12292
  387.4 26.9 %copy-start.31 = (s32[4096]{0:T(1024)S(1)}, s32[4096]{0:T(1024)}, u32[]{:S(2)}) copy-start(s32[4096]{0:T(1024)} %pad_clamp_fusion) | copy-start | bytes 49156
  394.0 575.7 %all-to-all-start = ((bf16[32,2,128]{2,1,0:T(2,128)(2,1)}), bf16[32,2,128]{2,1,0:T(2,128)(2,1)}, u32[]{:S(2)}, u32[]{:S(2)}) async-start(bf16[32,2,128]{2,1,0:T(2,128)(2,1)} %stack.3), calls=%async_computation | async-start | bytes 32768 | tf_op jit(solution)/shard_map/all_to_all | solution.py:183
  405.9 628.3 %all-reduce.22.cloned.1.call-start = ((), (), s32[]{:S(2)}) async-start(), calls=%async_computation.1 | async-start | bytes 1048576 | tf_op jit(solution)/shard_map/psum | solution.py:209
  927.0 23.3 %slice-start.6 = ((s8[8388608]{0:T(1024)(128)(4,1)}), s8[4194304]{0:T(1024)(128)(4,1)S(1)}, s32[]{:S(2)}) async-start(s8[8388608]{0:T(1024)(128)(4,1)} %bitcast.386), calls=%async_computation.8 | async-start | bytes 8388608
  979.1 56.3 %copy-start.2 = (f32[2,1024,256]{2,1,0:T(8,128)S(1)}, f32[2,1024,256]{2,1,0:T(8,128)}, u32[]{:S(2)}) copy-start(f32[2,1024,256]{2,1,0:T(8,128)} %param.19) | copy-start | bytes 6291460
  (61 other events, 686.6 us)
Sparse Core Ops, SparseCore 0:
  989.9 44.2 all-reduce.21
